TPU v7x, 32 devices: a whole 2x2x4 slice. The times are simulated.
32 devices in a mesh: groups: 2 (over y), row: 4 (over x, core), col: 4 (over z).
Axes of the slice: x: 2, y: 2, z: 4, core: 2. Of those that a mesh axis runs over, the one named last changes fastest.
Arguments:
- channels: bfloat16 [4, 16, 64, 8192], P('groups', None, 'row', 'col'), parts along dimension 0, may hold values from -6 to 6
- weights: float32 [32, 64], P('groups'), parts along dimension 0, may hold values from 0.25 to 4
- slab_in: float32 [2, 512, 8192], P(None, ('groups', 'row'), 'col'), parts along dimension 1, may hold values from -0.6 to 0.6
Outputs:
- slab_out: float32 [2, 512, 8192], P(None, ('groups', 'row'), 'col'), parts along dimension 1
There are 2 independent parts, one for each index of `groups`. A program takes and returns all parts, laid end to end along the dimension named above; each array names one. Nothing has to cross between parts.
All inputs are finite; a program needn't handle non-finite values.
Results may differ from a plain program's by a relative error of at most 0.0015.
Values may be sent and summed in bfloat16 or wider, within the bound.
A program may use at most 64 MiB of HBM per device.

v0:
```python
import jax
import jax.numpy as jnp
from jax import lax
from jax.sharding import PartitionSpec as P


def broadcast(value, axis, source):
    kept = jnp.where(lax.axis_index(axis) == source, value, 0).astype(value.dtype)
    return lax.psum(kept, axis)


def product(left_part, right_part):
    contract_dims = (((0, 1), (0, 1)), ((), ()))
    return lax.dot_general(left_part, right_part, contract_dims, preferred_element_type=jnp.float32)


def cross_terms(left_rows, right_cols):
    real_part = product(left_rows[0], right_cols[0]) + product(left_rows[1], right_cols[1])
    imag_part = product(left_rows[0], right_cols[1]) - product(left_rows[1], right_cols[0])
    return jnp.stack([real_part, imag_part])


def make_adder(weighted, portion):
    return cross_terms(weighted, portion)


def shards(channels, weights, slab_in):
    slab_count = slab_in.shape[1] * lax.axis_size("row")
    own_rows = channels[:, :, :, :slab_count]
    slab_piece = lax.all_to_all(own_rows, "row", split_axis=3, concat_axis=2, tiled=True)
    slab_piece = broadcast(slab_piece, "col", 0)
    weight_total = jnp.sum(weights)
    scaled = (weights / weight_total)[None, :, :, None]
    weighted = (slab_piece.astype(jnp.float32) * scaled).astype(jnp.bfloat16)
    increase = make_adder(weighted, lax.all_gather(channels, "row", axis=2, tiled=True))
    return slab_in + increase


def solution(mesh):
    return jax.shard_map(
        shards,
        mesh=mesh,
        in_specs=(
            P("groups", None, "row", "col"),
            P("groups", None),
            P(None, ("groups", "row"), "col"),
        ),
        out_specs=P(None, ("groups", "row"), "col"),
        check_vma=False,
    )
```

profile of v0, /device:TPU:24, one launch (start us, length us, event | category | flops | bytes accessed | tf_op | source)
XLA Modules:
  0.0 108.9 jit_solution(2065347155661065295)
XLA Ops:
  7.4 1.0 slice.19
  8.3 3.0 %copy.8 = bf16[2,16,16,256]{2,1,0,3:T(8,128)(2,1)S(1)} copy(bf16[2,16,16,256]{3,2,1,0:T(8,128)(2,1)S(1)} %slice.19) | data formatting | bytes 524288 | tf_op jit(solution)/shard_map/slice | solution.py:29
  11.3 2.9 %reshape.11 = bf16[4,2,16384]{2,1,0:T(2,128)(2,1)} reshape(bf16[256,2,16,16]{3,2,1,0:T(8,128)(2,1)S(1)} %bitcast.59) | data formatting | bytes 524288
  14.2 3.4 %all-to-all-start = ((bf16[4,2,16384]{2,1,0:T(2,128)(2,1)}), bf16[4,2,16384]{2,1,0:T(2,128)(2,1)S(1)}, u32[]{:S(2)}, u32[]{:S(2)}) async-start(bf16[4,2,16384]{2,1,0:T(2,128)(2,1)} %reshape.11), calls=%async_computation | async-start | bytes 524288 | tf_op jit(solution)/shard_map/all_to_all | solution.py:30
  17.6 0.0 all-reduce.2.cloned.1.call-start
  17.6 5.9 %all-to-all-done = bf16[4,2,16384]{2,1,0:T(2,128)(2,1)S(1)} async-done(((bf16[4,2,16384]{2,1,0:T(2,128)(2,1)}), bf16[4,2,16384]{2,1,0:T(2,128)(2,1)S(1)}, u32[]{:S(2)}, u32[]{:S(2)}) %all-to-all-start) | async-done | bytes 262176 | tf_op jit(solution)/shard_map/all_to_all | solution.py:30
  23.6 2.4 %reshape.12 = bf16[256,2,16,16]{3,2,1,0:T(8,128)(2,1)} reshape(bf16[4,2,16384]{2,1,0:T(2,128)(2,1)S(1)} %all-to-all-done) | data formatting | bytes 524288
  26.0 1.7 %broadcast_select_fusion = bf16[2,16,16,256]{2,1,0,3:T(8,128)(2,1)S(1)} fusion(pred[]{:T(512)S(6)} %eq.3, bf16[256,2,16,16]{3,2,1,0:T(8,128)(2,1)} %reshape.12), kind=kLoop, calls=%fused_computation.14 | loop fusion | flops 131072 | bytes 524289 | tf_op jit(solution)/shard_map/jit(_where)/select_n | solution.py:8
  27.7 0.0 copy-start.1
  27.7 2.3 %copy.12 = bf16[2,16,16,4,64]{4,3,2,1,0:T(4,128)(2,1)S(1)} copy(bf16[2,16,16,4,64]{2,1,0,4,3:T(8,128)(2,1)S(1)} %bitcast.58) | data formatting | bytes 524288 | tf_op jit(solution)/shard_map/jit(_where)/select_n | solution.py:8
  30.1 0.1 copy.10
  30.2 1.0 copy.11
  31.2 0.0 all-reduce.2.cloned.1.call-update
  31.2 0.0 all-gather.2.cloned.1.call-start
  31.2 0.5 all-gather.2.cloned.1.call-update
  31.8 0.0 copy-done.1
  31.8 0.6 reduce_sum.9
  32.4 0.6 broadcast_divide_fusion
  33.0 35.8 %all-reduce.2.cloned.1.call-done = bf16[2,16,64,64]{2,3,1,0:T(8,128)(2,1)} async-done(((bf16[2,16,64,64]{2,3,1,0:T(8,128)(2,1)}), bf16[2,16,64,64]{2,3,1,0:T(8,128)(2,1)}) %all-reduce.2.cloned.1.call-update) | async-done | bytes 262160 | tf_op jit(solution)/shard_map/psum | solution.py:9
  68.7 1.2 %multiply_convert_fusion = bf16[2,16,64,64]{2,3,1,0:T(8,128)(2,1)S(1)} fusion(bf16[2,16,64,64]{2,3,1,0:T(8,128)(2,1)} %all-reduce.2.cloned.1.call-done, f32[16,64]{1,0:T(8,128)S(1)} %broadcast_divide_fusion), kind=kLoop, calls=%fused_computation.16 | loop fusion | flops 393216 | bytes 528384 | tf_op jit(solution)/shard_map/convert_element_type | solution.py:34
  69.9 21.5 %all-gather.2.cloned.1.call-done = bf16[2,16,64,2048]{3,2,1,0:T(8,128)(2,1)} async-done(((bf16[2,16,16,2048]{3,2,1,0:T(8,128)(2,1)}), bf16[2,16,64,2048]{3,2,1,0:T(8,128)(2,1)}) %all-gather.2.cloned.1.call-update) | async-done | bytes 8388624 | tf_op jit(solution)/shard_map/all_gather | solution.py:35
  91.5 0.0 copy-start.2
  91.5 3.2 %fusion.4 = f32[64,2048]{1,0:T(8,128)S(1)} fusion(bf16[2,16,64,2048]{3,2,1,0:T(8,128)(2,1)} %all-gather.2.cloned.1.call-done, bf16[2,16,64,64]{2,3,1,0:T(8,128)(2,1)S(1)} %multiply_convert_fusion), kind=kOutput, calls=%fused_computation.6 | convolution fusion | flops 268435456 | bytes 4980736 | tf_op jit(solution)/shard_map/dot_general | solution.py:14
  94.7 3.5 %fusion.5 = f32[64,2048]{1,0:T(8,128)S(1)} fusion(bf16[2,16,64,2048]{3,2,1,0:T(8,128)(2,1)} %all-gather.2.cloned.1.call-done, bf16[2,16,64,64]{2,3,1,0:T(8,128)(2,1)S(1)} %multiply_convert_fusion), kind=kOutput, calls=%fused_computation.7 | convolution fusion | flops 268435456 | bytes 4980736 | tf_op jit(solution)/shard_map/dot_general | solution.py:14
  98.2 0.0 copy-done.2
  98.2 0.9 fusion.11
  99.1 0.0 copy-start
  99.1 0.9 fusion.9
  100.0 0.3 copy-done
  100.3 1.1 maximum_add_fusion
Async XLA Ops:
  14.2 9.4 %all-to-all-start = ((bf16[4,2,16384]{2,1,0:T(2,128)(2,1)}), bf16[4,2,16384]{2,1,0:T(2,128)(2,1)S(1)}, u32[]{:S(2)}, u32[]{:S(2)}) async-start(bf16[4,2,16384]{2,1,0:T(2,128)(2,1)} %reshape.11), calls=%async_computation | async-start | bytes 524288 | tf_op jit(solution)/shard_map/all_to_all | solution.py:30
  17.6 51.2 %all-reduce.2.cloned.1.call-start = ((), (), s32[]{:S(2)}) async-start(), calls=%async_computation.1 | async-start | bytes 1048576 | tf_op jit(solution)/shard_map/psum | solution.py:9
  27.7 4.0 %copy-start.1 = (f32[16,64]{1,0:T(8,128)S(1)}, f32[16,64]{1,0:T(8,128)}, u32[]{:S(2)}) copy-start(f32[16,64]{1,0:T(8,128)} %param.4) | copy-start | bytes 12292
  31.2 60.3 %all-gather.2.cloned.1.call-start = ((), (), s32[]{:S(2)}) async-start(), calls=%async_computation.2 | async-start | bytes 10485760 | tf_op jit(solution)/shard_map/all_gather | solution.py:35
  91.5 6.7 %copy-start.2 = (bf16[2,16,64,2048]{3,2,1,0:T(8,128)(2,1)S(1)}, bf16[2,16,64,2048]{3,2,1,0:T(8,128)(2,1)}, u32[]{:S(2)}) copy-start(bf16[2,16,64,2048]{3,2,1,0:T(8,128)(2,1)} %all-gather.2.cloned.1.call-done) | copy-start | bytes 25165828
  99.1 1.2 %copy-start = (f32[2,64,2048]{2,1,0:T(8,128)S(1)}, f32[2,64,2048]{2,1,0:T(8,128)}, u32[]{:S(2)}) copy-start(f32[2,64,2048]{2,1,0:T(8,128)} %param.5) | copy-start | bytes 3145732
Sparse Core Ops, SparseCore 0:
  31.3 37.3 all-reduce.1
Sparse Core Ops, SparseCore 1:
  33.2 58.2 all-gather.1
where the time goes:
time: 111 us; the launch traced here: 109 us
  waiting for transfers between devices  63.8 us (57%)
  between operations  15 us (14%)
  local copies, waits for them, and re-layouts  12.9 us (12%)
  matrix products  8.49 us (8%)
  other arithmetic  5.16 us (5%)
  starting transfers between devices  3.49 us (3%)
    psum x1, waiting for transfers between devices, broadcast(): return lax.psum(kept, axis)  35.8 us
    all_gather x1, waiting for transfers between devices, shards(): lax.all_gather(channels, 'row', axis=2, tiled=True)  21.5 us
    dot_general x4, matrix products, product(): lax.dot_general(left_part, right_part, contract_dims, preferred_element_t...  8.49 us
    all_to_all x1, waiting for transfers between devices, shards(): lax.all_to_all(own_rows, 'row', split_axis=3, concat_axis=2, tiled=True)  5.95 us
    unnamed x8, local copies, waits for them, and re-layouts  5.62 us
    slice x2, local copies, waits for them, and re-layouts, shards(): own_rows = channels[:, :, :, :slab_count]  3.92 us
    select_n x3, local copies, waits for them, and re-layouts, broadcast(): jnp.where(lax.axis_index(axis) == source, value, 0).astype(value.dtype)  3.41 us
    all_to_all x1, starting transfers between devices, shards(): lax.all_to_all(own_rows, 'row', split_axis=3, concat_axis=2, tiled=True)  3.41 us
  transfers between devices with their start and end apart: 3, of which 3 were waited for; matrix products, arithmetic and copies ran while one was open for 2% of the time, Pallas kernels for 0%

commit v1 on v0

v1 whole, which is shorter than its diff:
```python
import functools

import jax
import jax.numpy as jnp
from jax import lax
from jax.experimental import pallas as pl
from jax.experimental.pallas import tpu as pltpu
from jax.sharding import PartitionSpec as P

F32, BF16 = jnp.float32, jnp.bfloat16
MESH = pl.DeviceIdType.MESH


def kernel(
    chips, cols, blocks, direct, tile,
    channels, weights, slab, out,
    right, left, split, head, turned, total, sent, got,
    own_sem, pair_send, pair_recv, head_sem, slab_sem,
    left_send, left_recv, row_send, row_recv, out_sem,
):
    row, z = lax.axis_index("row"), lax.axis_index("col")
    x, c = row // 2, lax.rem(row, 2)
    pair = row + 1 - 2 * c
    depth, width = channels.shape[1:]
    rows = slab.shape[1]
    high = rows // blocks
    panels = weights.shape[0]
    samples = depth // panels
    tiles = width // tile
    steps = list(range(1, chips)) + [0]

    def peer(d):
        return 2 * lax.rem(x + d, chips) + c

    barrier = pltpu.get_barrier_semaphore()

    def greet(to_row, to_col):
        pl.semaphore_signal(barrier, 1, device_id={"row": to_row, "col": to_col}, device_id_type=MESH)

    greet(pair, z)
    for d in range(1, chips):
        greet(peer(d), z)

    @pl.when(z > 0)
    def _():
        greet(row, 0)
        greet(pair, 0)

    @pl.when(z > 1)
    def _():
        greet(row, z - 1)

    def head_copy(d):
        start = pl.multiple_of(lax.rem(x + d, chips) * (2 * rows), 2 * rows)
        return pltpu.make_async_copy(channels.at[:, :, pl.ds(start, 2 * rows)], head.at[d], head_sem.at[d])

    def own_copy(n):
        span = pl.ds(n * tile, tile)
        return pltpu.make_async_copy(channels.at[:, :, span], right.at[c, :, :, span], own_sem.at[n])

    def pair_copy(n, side):
        span = pl.ds(n * tile, tile)
        return pltpu.make_async_remote_copy(
            channels.at[:, :, span], right.at[side, :, :, span], pair_send.at[n], pair_recv.at[n],
            device_id={"row": pair, "col": z}, device_id_type=MESH)

    def left_copy(d, b, source, side, slot, to_row, to_col):
        return pltpu.make_async_remote_copy(
            source, left.at[d, b, side], left_send.at[d, b, slot], left_recv.at[d, b, side],
            device_id={"row": to_row, "col": to_col}, device_id_type=MESH)

    def row_copy(d, b):
        return pltpu.make_async_remote_copy(
            sent.at[d - 1, b], got.at[d - 1, b], row_send.at[d - 1, b], row_recv.at[d - 1, b],
            device_id={"row": peer(d), "col": z}, device_id_type=MESH)

    def out_copy(b):
        span = pl.ds(b * high, high)
        return pltpu.make_async_copy(total.at[:, span], out.at[:, span], out_sem.at[b])

    slab_copy = pltpu.make_async_copy(slab, total, slab_sem)

    @pl.when(z == 0)
    def _():
        for d in steps:
            head_copy(d).start()

    for n in range(tiles):
        own_copy(n).start()
    slab_copy.start()

    def head_sends(d, b):
        copies = [left_copy(d, b, split.at[d, 1 - c, b], c, 0, pair, z)]
        for far in (range(cols - 1, 0, -1) if direct and d else [1] if cols > 1 else []):
            copies.append(left_copy(d, b, split.at[d, c, b], c, 2 * far - 1, row, far))
            copies.append(left_copy(d, b, split.at[d, 1 - c, b], c, 2 * far, pair, far))
        return copies

    @pl.when(z == 0)
    def _():
        scaled = weights[...] / jnp.sum(weights[...])
        turned[...] = scaled.T
        mine = turned[pl.ds(pl.multiple_of(row * samples, samples), samples), :]
        gain = jnp.concatenate([jnp.broadcast_to(mine[:, p:p + 1], (samples, 2 * rows)) for p in range(panels)])
        for d in steps:
            head_copy(d).wait()
            for part in range(2):
                value = (head[d, part].astype(F32) * gain).T.astype(BF16)
                for side in range(2):
                    for b in range(blocks):
                        split[d, side, b, part] = value[side * rows + b * high:side * rows + (b + 1) * high]
            for b in range(blocks):
                left[d, b, c] = split[d, c, b]
            if d == steps[0]:
                pl.semaphore_wait(barrier, 2 * cols - 1 + chips - 1)
            for b in range(blocks):
                for copy in head_sends(d, b):
                    copy.start()
            if d == steps[0]:
                for n in range(tiles):
                    pair_copy(n, c).start()

    @pl.when(z > 0)
    def _():
        pl.semaphore_wait(barrier, 1 + chips - 1 + jnp.where(z < cols - 1, 1, 0))
        for n in range(tiles):
            pair_copy(n, c).start()

    def forwards(d):
        return not (direct and d)

    def take_left(d, b):
        @pl.when(z == 0)
        def _():
            left_copy(d, b, left.at[d, b, 1 - c], 1 - c, 0, pair, z).wait_recv()

        @pl.when(z > 0)
        def _():
            for side in range(2):
                left_copy(d, b, left.at[d, b, side], side, side, pair, z).wait_recv()
                if forwards(d):
                    @pl.when(z < cols - 1)
                    def _():
                        left_copy(d, b, left.at[d, b, side], side, side, row, z + 1).start()

    def multiply(d, b, first):
        real, imag = [], []
        for side in range(2):
            re, im = left[d, b, side, 0], left[d, b, side, 1]
            real += [re, im]
            imag += [-im, re]
        rows_in = jnp.concatenate([jnp.concatenate(real, axis=1), jnp.concatenate(imag, axis=1)], axis=0)

        def one(n):
            span = pl.ds(pl.multiple_of(n * tile, tile), tile)
            block = right[:, :, :, span].reshape(4 * depth, tile)
            value = jnp.dot(rows_in, block, preferred_element_type=F32).reshape(2, high, tile)
            if d:
                sent[d - 1, b, :, :, span] = value.astype(BF16)
            else:
                total[:, pl.ds(b * high, high), span] += value

        if first:
            for n in range(tiles):
                own_copy(n).wait()
                pair_copy(n, 1 - c).wait_recv()
                one(n)
        else:
            pl.loop(0, tiles)(one)

    first = True
    for d in steps:
        if d == 0:
            slab_copy.wait()
        for b in range(blocks):
            take_left(d, b)
            multiply(d, b, first)
            first = False
            if d:
                row_copy(d, b).start()

    for b in range(blocks):
        span = pl.ds(b * high, high)
        for d in range(1, chips):
            row_copy(d, b).wait_recv()
            total[:, span] += got[d - 1, b].astype(F32)
        out_copy(b).start()

    for n in range(tiles):
        pair_copy(n, c).wait_send()
    for d in range(1, chips):
        for b in range(blocks):
            row_copy(d, b).wait_send()

    @pl.when(z == 0)
    def _():
        for d in steps:
            for b in range(blocks):
                for copy in head_sends(d, b):
                    copy.wait_send()

    @pl.when((z > 0) & (z < cols - 1))
    def _():
        for d in steps:
            if forwards(d):
                for b in range(blocks):
                    for side in range(2):
                        left_copy(d, b, left.at[d, b, side], side, side, row, z + 1).wait_send()

    for b in range(blocks):
        out_copy(b).wait()


def shards(channels, weights, slab_in):
    chips, cols = lax.axis_size("row") // 2, lax.axis_size("col")
    _, panels, samples, width = channels.shape
    depth, rows = panels * samples, slab_in.shape[1]
    blocks, tile = 4, 512
    direct = cols <= 4
    high, tiles = rows // blocks, width // tile
    slots = 2 * cols if direct else 3
    others = max(chips - 1, 1)
    dma = pltpu.SemaphoreType.DMA
    hbm = pl.BlockSpec(memory_space=pl.ANY)
    return pl.pallas_call(
        functools.partial(kernel, chips, cols, blocks, direct, tile),
        out_shape=jax.ShapeDtypeStruct(slab_in.shape, F32),
        in_specs=[hbm, pl.BlockSpec(memory_space=pltpu.VMEM), hbm],
        out_specs=hbm,
        scratch_shapes=[
            pltpu.VMEM((2, 2, depth, width), BF16),
            pltpu.VMEM((chips, blocks, 2, 2, high, depth), BF16),
            pltpu.VMEM((chips, 2, blocks, 2, high, depth), BF16),
            pltpu.VMEM((chips, 2, depth, 2 * rows), BF16),
            pltpu.VMEM(weights.shape[::-1], F32),
            pltpu.VMEM(slab_in.shape, F32),
            pltpu.VMEM((others, blocks, 2, high, width), BF16),
            pltpu.VMEM((others, blocks, 2, high, width), BF16),
            dma((tiles,)), dma((tiles,)), dma((tiles,)), dma((chips,)), dma,
            dma((chips, blocks, slots)), dma((chips, blocks, 2)),
            dma((others, blocks)), dma((others, blocks)), dma((blocks,)),
        ],
        compiler_params=pltpu.CompilerParams(
            collective_id=0, has_side_effects=True, vmem_limit_bytes=40 * 2**20),
    )(channels.reshape(2, depth, width), weights, slab_in)


def solution(mesh):
    return jax.shard_map(
        shards,
        mesh=mesh,
        in_specs=(
            P("groups", None, "row", "col"),
            P("groups", None),
            P(None, ("groups", "row"), "col"),
        ),
        out_specs=P(None, ("groups", "row"), "col"),
        check_vma=False,
    )
```

time: 111 us -> 30.2 us (0.27); the launches traced: 109 us -> 30 us
  waiting for transfers between devices: 63.8 us -> 0 us
  Pallas kernels: 0 us -> 25.5 us
  between operations: 15 us -> 0.01 us
  matrix products: 8.49 us -> 0 us
  local copies, waits for them, and re-layouts: 12.9 us -> 4.48 us
  other arithmetic: 5.16 us -> 0 us
  starting transfers between devices: 3.49 us -> 0 us
    psum x1 -> x0, waiting for transfers between devices: 35.8 us -> none  [broadcast(): return lax.psum(kept, axis)]
    pallas_call x0 -> x1, Pallas kernels: none -> 25.5 us  [shards(): pl.pallas_call(functools.partial(kernel, chips, cols, blocks, direct, til...]
    all_gather x1 -> x0, waiting for transfers between devices: 21.5 us -> none  [shards(): lax.all_gather(channels, 'row', axis=2, tiled=True)]
    dot_general x4 -> x0, matrix products: 8.49 us -> none  [product(): lax.dot_general(left_part, right_part, contract_dims, preferred_element_t...]
    all_to_all x1 -> x0, waiting for transfers between devices: 5.95 us -> none  [shards(): lax.all_to_all(own_rows, 'row', split_axis=3, concat_axis=2, tiled=True)]
    slice x2 -> x0, local copies, waits for them, and re-layouts: 3.92 us -> none  [shards(): own_rows = channels[:, :, :, :slab_count]]
    select_n x3 -> x0, local copies, waits for them, and re-layouts: 3.41 us -> none  [broadcast(): jnp.where(lax.axis_index(axis) == source, value, 0).astype(value.dtype)]
    all_to_all x1 -> x0, starting transfers between devices: 3.41 us -> none  [shards(): lax.all_to_all(own_rows, 'row', split_axis=3, concat_axis=2, tiled=True)]
  transfers between devices with their start and end apart: 3 -> 0, of which waited for: 3 -> 0; matrix products, arithmetic and copies ran while one was open for 2% -> 0% of each run, Pallas kernels for 0% -> 0%
where the time goes in v1:
time: 30.2 us; the launch traced here: 30 us
  Pallas kernels  25.5 us (84%)
  local copies, waits for them, and re-layouts  4.48 us (15%)
    pallas_call x1, Pallas kernels, shards(): pl.pallas_call(functools.partial(kernel, chips, cols, blocks, direct, til...  25.5 us
    unnamed x7, local copies, waits for them, and re-layouts  4.48 us

profile of v1, /device:TPU:24, one launch (start us, length us, event | category | flops | bytes accessed | tf_op | source)
XLA Modules:
  0.0 30.0 jit_solution(18174479862462730895)
XLA Ops:
  0.0 0.0 copy-start
  0.0 1.6 %copy-done = bf16[2,16,16,2048]{3,2,1,0:T(8,128)(2,1)S(1)} copy-done((bf16[2,16,16,2048]{3,2,1,0:T(8,128)(2,1)S(1)}, bf16[2,16,16,2048]{3,2,1,0:T(8,128)(2,1)}, u32[]{:S(2)}) %copy-start) | copy-done | bytes 2097176
  1.6 0.0 copy-start.1
  1.6 1.2 %copy-done.1 = f32[2,64,2048]{2,1,0:T(8,128)S(1)} copy-done((f32[2,64,2048]{2,1,0:T(8,128)S(1)}, f32[2,64,2048]{2,1,0:T(8,128)}, u32[]{:S(2)}) %copy-start.1) | copy-done | bytes 1048600
  2.8 0.0 copy-start.2
  2.8 0.7 %copy-done.2 = f32[16,64]{1,0:T(8,128)S(1)} copy-done((f32[16,64]{1,0:T(8,128)S(1)}, f32[16,64]{1,0:T(8,128)}, u32[]{:S(2)}) %copy-start.2) | copy-done | bytes 4120
  3.5 25.5 %shard_map.37 = f32[2,64,2048]{2,1,0:T(8,128)S(1)} custom-call(bf16[2,256,2048]{2,1,0:T(8,128)(2,1)S(1)} %bitcast.1, f32[16,64]{1,0:T(8,128)S(1)} %copy-done.2, f32[2,64,2048]{2,1,0:T(8,128)S(1)} %copy-done.1), custom_call_target="tpu_custom_call" | custom-call | tf_op jit(solution)/shard_map/pallas_call | solution.py:225
  29.0 1.0 %copy.5 = f32[2,64,2048]{2,1,0:T(8,128)} copy(f32[2,64,2048]{2,1,0:T(8,128)S(1)} %shard_map.37) | data formatting | bytes 2097152
Async XLA Ops:
  0.0 1.6 %copy-start = (bf16[2,16,16,2048]{3,2,1,0:T(8,128)(2,1)S(1)}, bf16[2,16,16,2048]{3,2,1,0:T(8,128)(2,1)}, u32[]{:S(2)}) copy-start(bf16[2,16,16,2048]{3,2,1,0:T(8,128)(2,1)} %param.3) | copy-start | bytes 6291460
  1.6 1.2 %copy-start.1 = (f32[2,64,2048]{2,1,0:T(8,128)S(1)}, f32[2,64,2048]{2,1,0:T(8,128)}, u32[]{:S(2)}) copy-start(f32[2,64,2048]{2,1,0:T(8,128)} %slab.1) | copy-start | bytes 3145732
  2.8 0.7 %copy-start.2 = (f32[16,64]{1,0:T(8,128)S(1)}, f32[16,64]{1,0:T(8,128)}, u32[]{:S(2)}) copy-start(f32[16,64]{1,0:T(8,128)} %weights.1) | copy-start | bytes 12292

commit v2 on v1

v2 whole, which is shorter than its diff:
```python
import functools

import jax
import jax.numpy as jnp
from jax import lax
from jax.experimental import pallas as pl
from jax.experimental.pallas import tpu as pltpu
from jax.sharding import PartitionSpec as P

F32, BF16 = jnp.float32, jnp.bfloat16
MESH = pl.DeviceIdType.MESH


def kernel(
    chips, cols, blocks, tile,
    channels, weights, slab, total,
    right, left, split, head, gains, turned, sent, got,
    own_sem, pair_send, pair_recv, head_sem, gain_sem, slab_sem,
    left_send, left_recv, row_send, row_recv,
):
    row, z = lax.axis_index("row"), lax.axis_index("col")
    x, c = row // 2, lax.rem(row, 2)
    pair = row + 1 - 2 * c
    depth, width = channels.shape[1:]
    rows = slab.shape[1]
    high = rows // blocks
    panels = weights.shape[0]
    samples = depth // panels
    tiles = width // tile
    steps = list(range(1, chips)) + [0]

    def peer(d):
        return 2 * lax.rem(x + d, chips) + c

    barrier = pltpu.get_barrier_semaphore()

    def greet(to_row, to_col):
        pl.semaphore_signal(barrier, 1, device_id={"row": to_row, "col": to_col}, device_id_type=MESH)

    greet(pair, z)
    for d in range(1, chips):
        greet(peer(d), z)

    @pl.when(z > 0)
    def _():
        greet(row, z - 1)

    @pl.when(z == 1)
    def _():
        greet(pair, 0)

    def band(b):
        return pl.ds(b * high, high)

    def head_copy(d):
        start = pl.multiple_of(lax.rem(x + d, chips) * (2 * rows), 2 * rows)
        return pltpu.make_async_copy(channels.at[:, :, pl.ds(start, 2 * rows)], head.at[d], head_sem.at[d])

    def own_copy(n):
        span = pl.ds(n * tile, tile)
        return pltpu.make_async_copy(channels.at[:, :, span], right.at[c, :, :, span], own_sem.at[n])

    def pair_copy(n, side):
        span = pl.ds(n * tile, tile)
        return pltpu.make_async_remote_copy(
            channels.at[:, :, span], right.at[side, :, :, span], pair_send.at[n], pair_recv.at[n],
            device_id={"row": pair, "col": z}, device_id_type=MESH)

    def left_copy(d, b, source, side, slot, to_row, to_col):
        return pltpu.make_async_remote_copy(
            source.at[:, band(b)], left.at[d, side, :, band(b)], left_send.at[d, b, slot], left_recv.at[d, b, side],
            device_id={"row": to_row, "col": to_col}, device_id_type=MESH)

    def row_copy(d, b, n):
        span = pl.ds(pl.multiple_of(n * tile, tile), tile)
        return pltpu.make_async_remote_copy(
            sent.at[d - 1, :, band(b), span], got.at[d - 1, :, band(b), span],
            row_send.at[d - 1, b, n], row_recv.at[d - 1, b, n],
            device_id={"row": peer(d), "col": z}, device_id_type=MESH)

    slab_copy = pltpu.make_async_copy(slab, total, slab_sem)
    gain_copy = pltpu.make_async_copy(weights, gains, gain_sem)

    @pl.when(z == 0)
    def _():
        gain_copy.start()
        for d in steps:
            head_copy(d).start()

    for n in range(tiles):
        own_copy(n).start()
    slab_copy.start()

    order = [(d, b) for d in steps for b in range(blocks)]

    def send_next(count):
        for _ in range(count):
            if queue:
                d, b = queue.pop(0)

                @pl.when(z == 0)
                def _():
                    for copy in head_sends(d, b):
                        copy.start()

    def head_sends(d, b):
        copies = []
        if cols > 1:
            copies.append(left_copy(d, b, split.at[d, c], c, 1, row, 1))
            copies.append(left_copy(d, b, split.at[d, 1 - c], c, 2, pair, 1))
        return copies + [left_copy(d, b, split.at[d, 1 - c], c, 0, pair, z)]

    @pl.when(z == 0)
    def _():
        gain_copy.wait()
        scaled = gains[...] / jnp.sum(gains[...])
        turned[...] = scaled.T
        mine = turned[pl.ds(pl.multiple_of(row * samples, samples), samples), :]
        gain = jnp.concatenate([jnp.broadcast_to(mine[:, p:p + 1], (samples, 2 * rows)) for p in range(panels)])
        for d in steps:
            head_copy(d).wait()
            for part in range(2):
                value = (head[d, part].astype(F32) * gain).astype(BF16).T
                for side in range(2):
                    split[d, side, part] = value[side * rows:(side + 1) * rows]
            if d == steps[0]:
                pl.semaphore_wait(barrier, chips + (2 if cols > 1 else 0))
            if d == steps[0]:
                for copy in head_sends(*order[0]):
                    copy.start()
            if d == steps[0]:
                for n in range(tiles):
                    pair_copy(n, c).start()
            left[d, c] = split[d, c]
        for copy in head_sends(*order[0]):
            copy.wait_send()

    @pl.when(z > 0)
    def _():
        pl.semaphore_wait(barrier, 1 + chips - 1 + jnp.where(z < cols - 1, 1, 0))
        for n in range(tiles):
            pair_copy(n, c).start()

    def take_left(d, b):
        @pl.when(z == 0)
        def _():
            left_copy(d, b, left.at[d, 1 - c], 1 - c, 0, pair, z).wait_recv()

        @pl.when(z > 0)
        def _():
            for side in range(2):
                left_copy(d, b, left.at[d, side], side, side, pair, z).wait_recv()

                @pl.when(z < cols - 1)
                def _():
                    left_copy(d, b, left.at[d, side], side, side, row, z + 1).start()

    def multiply(d, low, size, first):
        real, imag = [], []
        for side in range(2):
            re, im = left[d, side, 0, low:low + size], left[d, side, 1, low:low + size]
            real += [re, im]
            imag += [-im, re]
        rows_in = jnp.concatenate([jnp.concatenate(real, axis=1), jnp.concatenate(imag, axis=1)], axis=0)

        def one(n):
            span = pl.ds(pl.multiple_of(n * tile, tile), tile)
            block = right[:, :, :, span].reshape(4 * depth, tile)
            value = jnp.dot(rows_in, block, preferred_element_type=F32).reshape(2, size, tile)
            if d:
                sent[d - 1, :, pl.ds(low, size), span] = value.astype(BF16)
                row_copy(d, low // high, n).start()
            else:
                total[:, pl.ds(low, size), span] += value

        if first:
            for n in range(tiles):
                own_copy(n).wait()
                pair_copy(n, 1 - c).wait_recv()
                one(n)
        else:
            pl.loop(0, tiles)(one)

    queue = order[1:]
    for d in steps[:-1]:
        for b in range(blocks):
            send_next(1 if b < 2 else 2)
            take_left(d, b)
            multiply(d, b * high, high, d == steps[0] and b == 0)
    send_next(len(queue))
    for b in range(blocks):
        take_left(0, b)
    slab_copy.wait()
    multiply(0, 0, rows, chips == 1)

    for b in range(blocks):
        for n in range(tiles):
            span = pl.ds(n * tile, tile)
            for d in range(1, chips):
                row_copy(d, b, n).wait_recv()
                total[:, band(b), span] += got[d - 1, :, band(b), span].astype(F32)

    for n in range(tiles):
        pair_copy(n, c).wait_send()
    for d in range(1, chips):
        for b in range(blocks):
            for n in range(tiles):
                row_copy(d, b, n).wait_send()

    @pl.when(z == 0)
    def _():
        for d, b in order[1:]:
            for copy in head_sends(d, b):
                copy.wait_send()

    @pl.when((z > 0) & (z < cols - 1))
    def _():
        for d in steps:
            for b in range(blocks):
                for side in range(2):
                    left_copy(d, b, left.at[d, side], side, side, row, z + 1).wait_send()

def shards(channels, weights, slab_in):
    chips, cols = lax.axis_size("row") // 2, lax.axis_size("col")
    _, panels, samples, width = channels.shape
    depth, rows = panels * samples, slab_in.shape[1]
    blocks, tile = 4, 512
    tiles = width // tile
    others = max(chips - 1, 1)
    dma = pltpu.SemaphoreType.DMA
    hbm = pl.BlockSpec(memory_space=pltpu.HBM)
    return pl.pallas_call(
        functools.partial(kernel, chips, cols, blocks, tile),
        out_shape=jax.ShapeDtypeStruct(slab_in.shape, F32),
        in_specs=[hbm, hbm, hbm],
        out_specs=pl.BlockSpec(memory_space=pltpu.VMEM),
        scratch_shapes=[
            pltpu.VMEM((2, 2, depth, width), BF16),
            pltpu.VMEM((chips, 2, 2, rows, depth), BF16),
            pltpu.VMEM((chips, 2, 2, rows, depth), BF16),
            pltpu.VMEM((chips, 2, depth, 2 * rows), BF16),
            pltpu.VMEM(weights.shape, F32),
            pltpu.VMEM(weights.shape[::-1], F32),
            pltpu.VMEM((others, 2, rows, width), BF16),
            pltpu.VMEM((others, 2, rows, width), BF16),
            dma((tiles,)), dma((tiles,)), dma((tiles,)), dma((chips,)), dma, dma,
            dma((chips, blocks, 3)), dma((chips, blocks, 2)),
            dma((others, blocks, tiles)), dma((others, blocks, tiles)),
        ],
        compiler_params=pltpu.CompilerParams(
            collective_id=0, has_side_effects=True, vmem_limit_bytes=52 * 2**20),
    )(channels.reshape(2, depth, width), weights, slab_in)


def solution(mesh):
    return jax.shard_map(
        shards,
        mesh=mesh,
        in_specs=(
            P("groups", None, "row", "col"),
            P("groups", None),
            P(None, ("groups", "row"), "col"),
        ),
        out_specs=P(None, ("groups", "row"), "col"),
        check_vma=False,
    )
```

time: 30.2 us -> 24.1 us (0.80)
  Pallas kernels: 25.5 us -> 22.3 us
  local copies, waits for them, and re-layouts: 4.48 us -> 1.67 us
    pallas_call x1, Pallas kernels: 25.5 us -> 22.3 us  [shards(): pl.pallas_call(functools.partial(kernel, chips, cols, blocks, tile), out_...]
    unnamed x7 -> x3, local copies, waits for them, and re-layouts: 4.48 us -> 1.67 us
where the time goes in v2:
time: 24.1 us; the launch traced here: 23.9 us
  Pallas kernels  22.3 us (93%)
  local copies, waits for them, and re-layouts  1.67 us (7%)
    pallas_call x1, Pallas kernels, shards(): pl.pallas_call(functools.partial(kernel, chips, cols, blocks, tile), out_...  22.3 us
    unnamed x3, local copies, waits for them, and re-layouts  1.67 us

profile of v2, /device:TPU:24, one launch (start us, length us, event | category | flops | bytes accessed | tf_op | source)
XLA Modules:
  0.0 23.9 jit_solution(2665840711770683851)
XLA Ops:
  0.0 0.0 copy-start
  0.0 0.7 %copy-done = f32[16,64]{1,0:T(8,128)S(1)} copy-done((f32[16,64]{1,0:T(8,128)S(1)}, f32[16,64]{1,0:T(8,128)}, u32[]{:S(2)}) %copy-start) | copy-done | bytes 4120
  0.7 22.3 %shard_map.37 = f32[2,64,2048]{2,1,0:T(8,128)S(1)} custom-call(bf16[2,256,2048]{2,1,0:T(8,128)(2,1)} %bitcast.1, f32[16,64]{1,0:T(8,128)S(1)} %copy-done, f32[2,64,2048]{2,1,0:T(8,128)} %slab.1), custom_call_target="tpu_custom_call" | custom-call | tf_op jit(solution)/shard_map/pallas_call | solution.py:232
  23.0 1.0 %copy.5 = f32[2,64,2048]{2,1,0:T(8,128)} copy(f32[2,64,2048]{2,1,0:T(8,128)S(1)} %shard_map.37) | data formatting | bytes 2097152
Async XLA Ops:
  0.0 0.7 %copy-start = (f32[16,64]{1,0:T(8,128)S(1)}, f32[16,64]{1,0:T(8,128)}, u32[]{:S(2)}) copy-start(f32[16,64]{1,0:T(8,128)} %weights.1) | copy-start | bytes 12292

commit v3 on v2

--- a/solution.py
+++ b/solution.py
@@ -229,6 +229,7 @@
     others = max(chips - 1, 1)
     dma = pltpu.SemaphoreType.DMA
     hbm = pl.BlockSpec(memory_space=pltpu.HBM)
+    operands = channels.reshape(2, depth, width), weights, slab_in
     return pl.pallas_call(
         functools.partial(kernel, chips, cols, blocks, tile),
         out_shape=jax.ShapeDtypeStruct(slab_in.shape, F32),
@@ -249,7 +250,7 @@
         ],
         compiler_params=pltpu.CompilerParams(
             collective_id=0, has_side_effects=True, vmem_limit_bytes=52 * 2**20),
-    )(channels.reshape(2, depth, width), weights, slab_in)
+    )(*(pltpu.with_memory_space_constraint(operand, pltpu.HBM) for operand in operands))
 
 
 def solution(mesh):

time: 24.1 us -> 23.5 us (0.975)
  local copies, waits for them, and re-layouts: 1.67 us -> 0.97 us
    unnamed x3 -> x1, local copies, waits for them, and re-layouts: 1.67 us -> 0.97 us
where the time goes in v3:
time: 23.5 us; the launch traced here: 23.3 us
  Pallas kernels  22.3 us (95%)
  local copies, waits for them, and re-layouts  0.97 us (4%)
    pallas_call x1, Pallas kernels, shards(): pl.pallas_call(functools.partial(kernel, chips, cols, blocks, tile), out_...  22.3 us
    unnamed x1, local copies, waits for them, and re-layouts  0.97 us

profile of v3, /device:TPU:24, one launch (start us, length us, event | category | flops | bytes accessed | tf_op | source)
XLA Modules:
  0.0 23.3 jit_solution(16681955679847936317)
XLA Ops:
  0.0 22.3 %shard_map.37 = f32[2,64,2048]{2,1,0:T(8,128)S(1)} custom-call(bf16[2,256,2048]{2,1,0:T(8,128)(2,1)} %bitcast.1, f32[16,64]{1,0:T(8,128)} %weights.1, f32[2,64,2048]{2,1,0:T(8,128)} %slab.1), custom_call_target="tpu_custom_call" | custom-call | tf_op jit(solution)/shard_map/pallas_call | solution.py:233
  22.4 1.0 %copy.5 = f32[2,64,2048]{2,1,0:T(8,128)} copy(f32[2,64,2048]{2,1,0:T(8,128)S(1)} %shard_map.37) | data formatting | bytes 2097152

commit v4 on v3

--- a/solution.py
+++ b/solution.py
@@ -184,7 +184,7 @@
     queue = order[1:]
     for d in steps[:-1]:
         for b in range(blocks):
-            send_next(1 if b < 2 else 2)
+            send_next(2)
             take_left(d, b)
             multiply(d, b * high, high, d == steps[0] and b == 0)
     send_next(len(queue))

time: 23.5 us -> 23.5 us (level)
  no operation moved by 1% of the time
where the time goes in v4:
time: 23.5 us; the launch traced here: 23.3 us
  Pallas kernels  22.3 us (95%)
  local copies, waits for them, and re-layouts  0.97 us (4%)
    pallas_call x1, Pallas kernels, shards(): pl.pallas_call(functools.partial(kernel, chips, cols, blocks, tile), out_...  22.3 us
    unnamed x1, local copies, waits for them, and re-layouts  0.97 us

profile of v4, /device:TPU:24, one launch (start us, length us, event | category | flops | bytes accessed | tf_op | source)
XLA Modules:
  0.0 23.3 jit_solution(1705238121769276776)
XLA Ops:
  0.0 22.3 %shard_map.37 = f32[2,64,2048]{2,1,0:T(8,128)S(1)} custom-call(bf16[2,256,2048]{2,1,0:T(8,128)(2,1)} %bitcast.1, f32[16,64]{1,0:T(8,128)} %weights.1, f32[2,64,2048]{2,1,0:T(8,128)} %slab.1), custom_call_target="tpu_custom_call" | custom-call | tf_op jit(solution)/shard_map/pallas_call | solution.py:233
  22.4 1.0 %copy.5 = f32[2,64,2048]{2,1,0:T(8,128)} copy(f32[2,64,2048]{2,1,0:T(8,128)S(1)} %shard_map.37) | data formatting | bytes 2097152

commit v5 on v4

--- a/solution.py
+++ b/solution.py
@@ -224,7 +224,7 @@
     chips, cols = lax.axis_size("row") // 2, lax.axis_size("col")
     _, panels, samples, width = channels.shape
     depth, rows = panels * samples, slab_in.shape[1]
-    blocks, tile = 4, 512
+    blocks, tile = 4, 1024
     tiles = width // tile
     others = max(chips - 1, 1)
     dma = pltpu.SemaphoreType.DMA

time: 23.5 us -> 23.3 us (level)
  no operation moved by 1% of the time
where the time goes in v5:
time: 23.3 us; the launch traced here: 23.2 us
  Pallas kernels  22.2 us (95%)
  local copies, waits for them, and re-layouts  0.97 us (4%)
    pallas_call x1, Pallas kernels, shards(): pl.pallas_call(functools.partial(kernel, chips, cols, blocks, tile), out_...  22.2 us
    unnamed x1, local copies, waits for them, and re-layouts  0.97 us

profile of v5, /device:TPU:24, one launch (start us, length us, event | category | flops | bytes accessed | tf_op | source)
XLA Modules:
  0.0 23.2 jit_solution(17636464052167661824)
XLA Ops:
  0.0 22.2 %shard_map.37 = f32[2,64,2048]{2,1,0:T(8,128)S(1)} custom-call(bf16[2,256,2048]{2,1,0:T(8,128)(2,1)} %bitcast.1, f32[16,64]{1,0:T(8,128)} %weights.1, f32[2,64,2048]{2,1,0:T(8,128)} %slab.1), custom_call_target="tpu_custom_call" | custom-call | tf_op jit(solution)/shard_map/pallas_call | solution.py:233
  22.2 1.0 %copy.5 = f32[2,64,2048]{2,1,0:T(8,128)} copy(f32[2,64,2048]{2,1,0:T(8,128)S(1)} %shard_map.37) | data formatting | bytes 2097152
